TPU v7x, 32 devices: a whole 2x2x4 slice. The times are simulated.
32 devices in a mesh: rec: 16 (over z, y, x), var: 2 (over core).
Axes of the slice: x: 2, y: 2, z: 4, core: 2. Of those that a mesh axis runs over, the one named last changes fastest.
Arguments:
- records: bfloat16 [32768, 8192], P('rec', 'var'), as said below
- test_matrix: bfloat16 [8192, 256], P('var'), may hold values from -0.0625 to 0.0625
- col_types: int32 [8192], P('var'), may hold values from 0 to 1
- col_groups: int32 [8192], P('var'), may hold values from 0 to 15
- group_weight: float32 [16], replicated, may hold values from 0.5 to 2
Outputs:
- scores_basis: bfloat16 [32768, 256], P(('rec', 'var'))
- projection: bfloat16 [256, 8192], P(None, 'var')
Inputs may be any that keep to these rules, and one draw needn't show every extreme that they name: `records`: every entry is positive.
All inputs are finite; a program needn't handle non-finite values.
Results may differ from a plain program's by a relative error of at most 0.0043.
The roundings to bfloat16 on the way count: a program that leaves them out, or rounds other values in their place, can miss the bound.
Values sent between devices are 32-bit elements; how exact they have to be, the bound alone decides.
A program may use at most 64 MiB of HBM per device.

v0:
```python
import math
import jax
import jax.numpy as jnp
from jax import lax
from jax.sharding import PartitionSpec as P

epsilon = 1e-05
highest = lax.Precision.HIGHEST


def column_factor(col_mean, col_square, col_types, col_weight):
    spread = col_square - col_mean * col_mean
    picked = jnp.where(col_types == 1, lax.rsqrt(col_mean + epsilon), lax.rsqrt(spread + epsilon))
    return picked * col_weight


def row_gram(left, right):
    return lax.dot_general(
        left, right, (((1,), (1,)), ((), ())), precision=highest, preferred_element_type=jnp.float32
    )


def lower_solve(lower, right):
    return lax.linalg.triangular_solve(lower, right, left_side=True, lower=True)


def local(records, test_matrix, col_types, col_groups, group_weight):
    total_rows = records.shape[0] * lax.axis_size("rec")
    values = records.astype(jnp.float32)
    col_sum, col_square = lax.psum((jnp.sum(values, 0), jnp.sum(values * values, 0)), "rec")
    col_mean = col_sum / total_rows
    onehot = (
        col_groups[:, None] == jnp.arange(group_weight.shape[0], dtype=jnp.int32)[None, :]
    ).astype(jnp.float32)
    col_weight = jnp.dot(onehot, group_weight, precision=highest)
    factor = column_factor(col_mean, col_square / total_rows, col_types, col_weight)
    scaled = ((values - col_mean) * factor).astype(jnp.bfloat16)
    partial_sketch = lax.dot_general(
        test_matrix, scaled, (((0,), (1,)), ((), ())), preferred_element_type=jnp.float32
    )
    piece_len = records.shape[0] // lax.axis_size("var")
    sketch = lax.psum(partial_sketch, "var")
    own_rows = lax.dynamic_slice_in_dim(sketch, lax.axis_index("var") * piece_len, piece_len, 1)
    factor_lower = jnp.linalg.cholesky(lax.psum(row_gram(own_rows, own_rows), ("rec", "var")))
    basis_own = lower_solve(factor_lower, own_rows)
    whole_basis = lower_solve(factor_lower, sketch)
    result = jnp.dot(whole_basis, scaled, precision=highest, preferred_element_type=jnp.float32)
    summed = lax.psum(result, "rec")
    summed = summed / math.sqrt(total_rows)
    scores_basis = (basis_own.T * math.sqrt(total_rows)).astype(jnp.bfloat16)
    return (scores_basis, summed.astype(jnp.bfloat16))


def solution(mesh):
    in_specs = (P("rec", "var"), P("var", None), P("var"), P("var"), P())
    out_specs = (P(("rec", "var"), None), P(None, "var"))
    return jax.shard_map(local, mesh=mesh, in_specs=in_specs, out_specs=out_specs, check_vma=False)
```

profile of v0, /device:TPU:0, one launch (start us, length us, event | category | flops | bytes accessed | tf_op | source)
XLA Modules:
  0.0 518.7 jit_solution(11401620359540813519)
XLA Ops:
  7.2 0.0 copy-start
  7.2 0.0 copy-start.3
  7.2 0.0 copy-start.2
  7.2 0.0 copy-start.1
  7.2 0.0 all-reduce.6.cloned.1.call-start
  7.3 7.7 %convert_reduce_fusion = (f32[4096]{0:T(1024)S(1)}, f32[4096]{0:T(1024)S(1)}) fusion(bf16[2048,4096]{1,0:T(8,128)(2,1)} %param.5), kind=kLoop, calls=%fused_computation.4 | loop fusion | flops 33546240 | bytes 16809984 | tf_op jit(solution)/shard_map/reduce_sum | solution.py:30
  15.0 0.0 copy-done.3
  15.0 0.0 copy-done.2
  15.0 0.2 fusion.22
  15.2 78.6 %all-reduce.1 = (f32[4096]{0:T(1024)S(1)}, f32[4096]{0:T(1024)S(1)}) all-reduce(f32[4096]{0:T(1024)S(1)} %get-tuple-element.15, f32[4096]{0:T(1024)S(1)} %get-tuple-element.14), channel_id=1, replica_groups=mesh['rec'=16,'var'=2] {'rec'}, use_global_device_ids=true, to_apply=%region_3.0 | all-reduce | flops 8192 | bytes 65536 | tf_op jit(solution)/shard_map/psum | solution.py:30
  93.8 0.0 copy-done.1
  93.8 0.0 copy-done
  93.8 9.9 %fusion.7 = f32[256,2048]{0,1:T(8,128)} fusion(bf16[4096,256]{1,0:T(8,128)(2,1)S(1)} %copy-done, bf16[2048,4096]{1,0:T(8,128)(2,1)} %param.5, f32[4096]{0:T(1024)S(1)} %get-tuple-element.33, f32[4096]{0:T(1024)S(1)} %get-tuple-element.32), kind=kOutput, calls=%fused_computation.11 | convolution fusion | flops 4328521728 | bytes 21004288 | tf_op jit(solution)/shard_map/dot_general | solution.py:38
  103.7 0.0 all-reduce.6.cloned.1.call-update
  103.7 0.0 all-reduce.8.cloned.1.call-start
  103.8 17.2 %all-reduce.6.cloned.1.call-done = f32[256,2048]{0,1:T(8,128)} async-done(((f32[256,2048]{0,1:T(8,128)}), f32[256,2048]{0,1:T(8,128)}) %all-reduce.6.cloned.1.call-update) | async-done | bytes 2097168 | tf_op jit(solution)/shard_map/psum | solution.py:42
  120.9 4.2 fusion.16
  125.2 0.0 all-reduce.8.cloned.1.call-update
  125.2 0.2 all-reduce.10.cloned.1.call-start
  125.5 128.7 %all-reduce.8.cloned.1.call-done = f32[256,256]{0,1:T(8,128)} async-done(((f32[256,256]{0,1:T(8,128)}), f32[256,256]{0,1:T(8,128)}) %all-reduce.8.cloned.1.call-update) | async-done | bytes 262160 | tf_op jit(solution)/shard_map/psum | solution.py:44
  254.2 1.1 copy.11
  255.3 1.0 fusion.21
  256.3 11.7 %cholesky.50 = f32[128,128]{1,0:T(8,128)S(1)} custom-call(f32[128,128]{1,0:T(8,128)S(1)} %cholesky.118), custom_call_target="Cholesky" | custom-call | tf_op jit(solution)/shard_map/jit(cholesky)/cholesky | solution.py:44
  268.0 9.8 %custom-call.16 = f32[1,128,128]{1,2,0:T(8,128)S(1)} custom-call(f32[1,128,128]{2,1,0:T(8,128)S(1)} %get-tuple-element.31), custom_call_target="InvertDiagBlocksLowerTriangular" | custom-call | tf_op jit(solution)/shard_map/jit(cholesky)/cholesky | solution.py:44
  277.9 0.2 constant_dynamic-update-slice_fusion
  278.1 0.3 convolution_subtract_fusion.2
  278.4 11.7 %cholesky.105 = f32[128,128]{1,0:T(8,128)S(1)} custom-call(f32[128,128]{1,0:T(8,128)S(1)} %convolution_subtract_fusion.2), custom_call_target="Cholesky" | custom-call | tf_op jit(solution)/shard_map/jit(cholesky)/cholesky | solution.py:44
  290.1 0.7 compare_reduce_fusion
  292.2 0.1 triangular_solve.72
  292.3 4.3 while.1
  292.5 0.6 fusion.44
  293.1 1.4 bitcast_dynamic-update-slice_fusion.2
  294.5 0.6 fusion.44
  295.1 1.4 bitcast_dynamic-update-slice_fusion.2
  296.6 19.7 %custom-call.17 = f32[2,128,128]{1,2,0:T(8,128)S(1)} custom-call(f32[2,128,128]{2,1,0:T(8,128)S(1)} %get-tuple-element.9), custom_call_target="InvertDiagBlocksLowerTriangular" | custom-call | tf_op jit(solution)/shard_map/triangular_solve | solution.py:24
  316.3 2.3 fusion.13
  318.6 3.0 convolution_subtract_fusion
  321.6 1.1 fusion.27
  322.7 18.2 %fusion.3 = f32[256,4096]{1,0:T(8,128)} fusion(bf16[2048,4096]{1,0:T(8,128)(2,1)} %param.5, f32[4096]{0:T(1024)S(1)} %get-tuple-element.33, f32[4096]{0:T(1024)S(1)} %get-tuple-element.32, f32[128,2048]{1,0:T(8,128)S(1)} %fusion.27, f32[128,2048]{1,0:T(8,128)S(1)} %fusion.13), kind=kOutput, calls=%fused_computation.8 | convolution fusion | flops 25803882496 | bytes 23101440 | tf_op jit(solution)/shard_map/dot_general | solution.py:47
  340.9 0.0 all-reduce.10.cloned.1.call-update
  340.9 1.7 fusion.19
  342.6 2.0 convolution_subtract_fusion.1
  344.7 0.6 fusion.28
  345.3 0.1 fusion.18
  345.4 1.0 copy.12
  346.4 161.8 %all-reduce.10.cloned.1.call-done = f32[256,4096]{1,0:T(8,128)} async-done(((f32[256,4096]{1,0:T(8,128)}), f32[256,4096]{1,0:T(8,128)}) %all-reduce.10.cloned.1.call-update) | async-done | bytes 4194320 | tf_op jit(solution)/shard_map/psum | solution.py:48
  508.3 3.9 multiply_convert_fusion
  (10 shorter events, 0.2 us)
Async XLA Ops:
  7.2 86.6 %copy-start = (bf16[4096,256]{1,0:T(8,128)(2,1)S(1)}, bf16[4096,256]{1,0:T(8,128)(2,1)}, u32[]{:S(2)}) copy-start(bf16[4096,256]{1,0:T(8,128)(2,1)} %param.6) | copy-start | bytes 6291460
  7.2 7.8 %copy-start.3 = (f32[16]{0:T(128)S(1)}, f32[16]{0:T(128)}, u32[]{:S(2)}) copy-start(f32[16]{0:T(128)} %param.9) | copy-start | bytes 196
  7.2 7.8 %copy-start.2 = (s32[4096]{0:T(1024)S(1)}, s32[4096]{0:T(1024)}, u32[]{:S(2)}) copy-start(s32[4096]{0:T(1024)} %param.8) | copy-start | bytes 49156
  7.2 86.6 %copy-start.1 = (s32[4096]{0:T(1024)S(1)}, s32[4096]{0:T(1024)}, u32[]{:S(2)}) copy-start(s32[4096]{0:T(1024)} %param.7) | copy-start | bytes 49156
  7.2 113.7 %all-reduce.6.cloned.1.call-start = ((), (), s32[]{:S(2)}) async-start(), calls=%async_computation | async-start | bytes 4194304 | tf_op jit(solution)/shard_map/psum | solution.py:42
  103.7 150.5 %all-reduce.8.cloned.1.call-start = ((), (), s32[]{:S(2)}) async-start(), calls=%async_computation.1 | async-start | bytes 524288 | tf_op jit(solution)/shard_map/psum | solution.py:44
  125.2 383.1 %all-reduce.10.cloned.1.call-start = ((), (), s32[]{:S(2)}) async-start(), calls=%async_computation.2 | async-start | bytes 8388608 | tf_op jit(solution)/shard_map/psum | solution.py:48
Sparse Core Ops, SparseCore 0:
  103.8 17.0 all-reduce.5
  127.9 126.2 all-reduce.7
  341.1 167.1 all-reduce.9
where the time goes:
time: 519 us
  waiting for transfers between devices  308 us (59%)
  blocking collectives  78.6 us (15%)
  other arithmetic  66.4 us (13%)
  matrix products  43.8 us (8%)
  between operations  15.3 us (3%)
  local copies, waits for them, and re-layouts  6.25 us (1%)
    psum x1, waiting for transfers between devices, local(): summed = lax.psum(result, 'rec')  162 us
    psum x1, waiting for transfers between devices, local(): lax.psum(row_gram(own_rows, own_rows), ('rec', 'var'))  129 us
    psum x1, blocking collectives, local(): lax.psum((jnp.sum(values, 0), jnp.sum(values * values, 0)), 'rec')  78.6 us
    another operation x6, other arithmetic, local(): jnp.linalg.cholesky(lax.psum(row_gram(own_rows, own_rows), ('rec', 'var')))  34 us
    another operation x3, other arithmetic, lower_solve(): return lax.linalg.triangular_solve(lower, right, left_side=True, lower=True)  19.7 us
    dot_general x1, matrix products, local(): jnp.dot(whole_basis, scaled, precision=highest, preferred_element_type=jn...  18.2 us
    psum x1, waiting for transfers between devices, local(): sketch = lax.psum(partial_sketch, 'var')  17.2 us
    another operation x6, matrix products, lower_solve(): return lax.linalg.triangular_solve(lower, right, left_side=True, lower=True)  10.8 us
  transfers between devices with their start and end apart: 3, of which 3 were waited for; matrix products, arithmetic and copies ran while one was open for 1% of the time, Pallas kernels for 0%

commit v1 on v0

--- a/solution.py
+++ b/solution.py
@@ -1,3 +1,4 @@
+import functools
 import math
 import jax
 import jax.numpy as jnp
@@ -6,6 +7,13 @@
 
 epsilon = 1e-05
 highest = lax.Precision.HIGHEST
+
+
+def _extend_figure(z_in, mesh_name):
+    return jnp.sum(jax.lax.all_gather(z_in, mesh_name), 0)
+
+
+process_teams_all = functools.partial(_extend_figure, mesh_name=("rec", "var"))
 
 
 def column_factor(col_mean, col_square, col_types, col_weight):
@@ -41,7 +49,7 @@
     piece_len = records.shape[0] // lax.axis_size("var")
     sketch = lax.psum(partial_sketch, "var")
     own_rows = lax.dynamic_slice_in_dim(sketch, lax.axis_index("var") * piece_len, piece_len, 1)
-    factor_lower = jnp.linalg.cholesky(lax.psum(row_gram(own_rows, own_rows), ("rec", "var")))
+    factor_lower = jnp.linalg.cholesky(process_teams_all(row_gram(own_rows, own_rows)))
     basis_own = lower_solve(factor_lower, own_rows)
     whole_basis = lower_solve(factor_lower, sketch)
     result = jnp.dot(whole_basis, scaled, precision=highest, preferred_element_type=jnp.float32)

time: 519 us -> 471 us (0.908)
  waiting for transfers between devices: 308 us -> 257 us
    psum x1 -> x0, waiting for transfers between devices: 129 us -> none  [local(): lax.psum(row_gram(own_rows, own_rows), ('rec', 'var'))]
    all_gather x0 -> x1, waiting for transfers between devices: none -> 78.5 us  [_extend_figure(): return jnp.sum(jax.lax.all_gather(z_in, mesh_name), 0)]
where the time goes in v1:
time: 471 us; the launch traced here: 470 us
  waiting for transfers between devices  257 us (55%)
  blocking collectives  78.6 us (17%)
  other arithmetic  69.4 us (15%)
  matrix products  43.8 us (9%)
  between operations  15.3 us (3%)
  local copies, waits for them, and re-layouts  5.3 us (1%)
    psum x1, waiting for transfers between devices, local(): summed = lax.psum(result, 'rec')  161 us
    psum x1, blocking collectives, local(): lax.psum((jnp.sum(values, 0), jnp.sum(values * values, 0)), 'rec')  78.6 us
    all_gather x1, waiting for transfers between devices, _extend_figure(): return jnp.sum(jax.lax.all_gather(z_in, mesh_name), 0)  78.5 us
    another operation x6, other arithmetic, local(): jnp.linalg.cholesky(process_teams_all(row_gram(own_rows, own_rows)))  34 us
    another operation x3, other arithmetic, lower_solve(): return lax.linalg.triangular_solve(lower, right, left_side=True, lower=True)  19.7 us
    dot_general x1, matrix products, local(): jnp.dot(whole_basis, scaled, precision=highest, preferred_element_type=jn...  18.2 us
    psum x1, waiting for transfers between devices, local(): sketch = lax.psum(partial_sketch, 'var')  17.2 us
    another operation x6, matrix products, lower_solve(): return lax.linalg.triangular_solve(lower, right, left_side=True, lower=True)  10.8 us
  transfers between devices with their start and end apart: 3, of which 3 were waited for; matrix products, arithmetic and copies ran while one was open for 1% of the time, Pallas kernels for 0%

profile of v1, /device:TPU:0, one launch (start us, length us, event | category | flops | bytes accessed | tf_op | source)
XLA Modules:
  0.0 470.1 jit_solution(17558287568567297276)
XLA Ops:
  7.2 0.0 copy-start
  7.2 0.0 copy-start.2
  7.2 0.0 copy-start.3
  7.2 0.0 copy-start.1
  7.2 0.0 all-reduce.5.cloned.1.call-start
  7.3 7.7 %convert_reduce_fusion = (f32[4096]{0:T(1024)S(1)}, f32[4096]{0:T(1024)S(1)}) fusion(bf16[2048,4096]{1,0:T(8,128)(2,1)} %param.5), kind=kLoop, calls=%fused_computation.4 | loop fusion | flops 33546240 | bytes 16809984 | tf_op jit(solution)/shard_map/reduce_sum | solution.py:38
  15.0 78.6 %all-reduce.1 = (f32[4096]{0:T(1024)S(1)}, f32[4096]{0:T(1024)S(1)}) all-reduce(f32[4096]{0:T(1024)S(1)} %get-tuple-element.17, f32[4096]{0:T(1024)S(1)} %get-tuple-element.16), channel_id=1, replica_groups=mesh['rec'=16,'var'=2] {'rec'}, use_global_device_ids=true, to_apply=%region_3.0 | all-reduce | flops 8192 | bytes 65536 | tf_op jit(solution)/shard_map/psum | solution.py:38
  93.5 0.0 copy-done.2
  93.5 0.0 copy-done.3
  93.6 0.2 fusion.22
  93.8 0.0 copy-done.1
  93.8 0.0 copy-done
  93.8 9.9 %fusion.7 = f32[256,2048]{0,1:T(8,128)} fusion(bf16[4096,256]{1,0:T(8,128)(2,1)S(1)} %copy-done, bf16[2048,4096]{1,0:T(8,128)(2,1)} %param.5, f32[4096]{0:T(1024)S(1)} %get-tuple-element.35, f32[4096]{0:T(1024)S(1)} %get-tuple-element.34), kind=kOutput, calls=%fused_computation.11 | convolution fusion | flops 4328521728 | bytes 21004288 | tf_op jit(solution)/shard_map/dot_general | solution.py:46
  103.7 0.0 all-reduce.5.cloned.1.call-update
  103.7 0.0 all-gather.3.cloned.1.call-start
  103.8 17.2 %all-reduce.5.cloned.1.call-done = f32[256,2048]{0,1:T(8,128)} async-done(((f32[256,2048]{0,1:T(8,128)}), f32[256,2048]{0,1:T(8,128)}) %all-reduce.5.cloned.1.call-update) | async-done | bytes 2097168 | tf_op jit(solution)/shard_map/psum | solution.py:50
  121.0 4.3 fusion.16
  125.2 0.0 all-gather.3.cloned.1.call-update
  125.2 0.2 all-reduce.7.cloned.1.call-start
  125.5 78.5 %all-gather.3.cloned.1.call-done = f32[8192,256]{1,0:T(8,128)} async-done(((f32[256,256]{1,0:T(8,128)}), f32[8192,256]{1,0:T(8,128)}) %all-gather.3.cloned.1.call-update) | async-done | bytes 8388624 | tf_op jit(solution)/shard_map/all_gather | solution.py:13
  204.0 3.9 reduce_sum.29
  207.9 0.1 copy.11
  208.1 11.7 %cholesky.50 = f32[128,128]{1,0:T(8,128)S(1)} custom-call(f32[128,128]{1,0:T(8,128)S(1)} %cholesky.118), custom_call_target="Cholesky" | custom-call | tf_op jit(solution)/shard_map/jit(cholesky)/cholesky | solution.py:52
  219.9 9.8 %custom-call.16 = f32[1,128,128]{1,2,0:T(8,128)S(1)} custom-call(f32[1,128,128]{2,1,0:T(8,128)S(1)} %get-tuple-element.33), custom_call_target="InvertDiagBlocksLowerTriangular" | custom-call | tf_op jit(solution)/shard_map/jit(cholesky)/cholesky | solution.py:52
  229.7 0.2 constant_dynamic-update-slice_fusion
  229.9 0.3 convolution_subtract_fusion.2
  230.2 11.7 %cholesky.105 = f32[128,128]{1,0:T(8,128)S(1)} custom-call(f32[128,128]{1,0:T(8,128)S(1)} %convolution_subtract_fusion.2), custom_call_target="Cholesky" | custom-call | tf_op jit(solution)/shard_map/jit(cholesky)/cholesky | solution.py:52
  241.9 0.7 compare_reduce_fusion
  244.0 0.1 triangular_solve.72
  244.1 4.3 while.1
  244.3 0.6 fusion.44
  244.9 1.4 bitcast_dynamic-update-slice_fusion.2
  246.3 0.6 fusion.44
  246.9 1.4 bitcast_dynamic-update-slice_fusion.2
  248.4 19.7 %custom-call.17 = f32[2,128,128]{1,2,0:T(8,128)S(1)} custom-call(f32[2,128,128]{2,1,0:T(8,128)S(1)} %get-tuple-element.9), custom_call_target="InvertDiagBlocksLowerTriangular" | custom-call | tf_op jit(solution)/shard_map/triangular_solve | solution.py:32
  268.1 2.3 fusion.13
  270.4 3.0 convolution_subtract_fusion
  273.4 1.1 fusion.27
  274.5 18.2 %fusion.3 = f32[256,4096]{1,0:T(8,128)} fusion(bf16[2048,4096]{1,0:T(8,128)(2,1)} %param.5, f32[4096]{0:T(1024)S(1)} %get-tuple-element.35, f32[4096]{0:T(1024)S(1)} %get-tuple-element.34, f32[128,2048]{1,0:T(8,128)S(1)} %fusion.27, f32[128,2048]{1,0:T(8,128)S(1)} %fusion.13), kind=kOutput, calls=%fused_computation.8 | convolution fusion | flops 25803882496 | bytes 23101440 | tf_op jit(solution)/shard_map/dot_general | solution.py:55
  292.7 0.0 all-reduce.7.cloned.1.call-update
  292.7 1.7 fusion.19
  294.4 2.0 convolution_subtract_fusion.1
  296.5 0.6 fusion.28
  297.1 0.1 fusion.18
  297.2 1.0 copy.14
  298.2 161.4 %all-reduce.7.cloned.1.call-done = f32[256,4096]{1,0:T(8,128)} async-done(((f32[256,4096]{1,0:T(8,128)}), f32[256,4096]{1,0:T(8,128)}) %all-reduce.7.cloned.1.call-update) | async-done | bytes 4194320 | tf_op jit(solution)/shard_map/psum | solution.py:56
  459.7 3.9 multiply_convert_fusion
  (11 shorter events, 0.2 us)
Async XLA Ops:
  7.2 86.6 %copy-start = (bf16[4096,256]{1,0:T(8,128)(2,1)S(1)}, bf16[4096,256]{1,0:T(8,128)(2,1)}, u32[]{:S(2)}) copy-start(bf16[4096,256]{1,0:T(8,128)(2,1)} %param.6) | copy-start | bytes 6291460
  7.2 86.4 %copy-start.2 = (s32[4096]{0:T(1024)S(1)}, s32[4096]{0:T(1024)}, u32[]{:S(2)}) copy-start(s32[4096]{0:T(1024)} %param.8) | copy-start | bytes 49156
  7.2 86.4 %copy-start.3 = (f32[16]{0:T(128)S(1)}, f32[16]{0:T(128)}, u32[]{:S(2)}) copy-start(f32[16]{0:T(128)} %param.9) | copy-start | bytes 196
  7.2 86.6 %copy-start.1 = (s32[4096]{0:T(1024)S(1)}, s32[4096]{0:T(1024)}, u32[]{:S(2)}) copy-start(s32[4096]{0:T(1024)} %param.7) | copy-start | bytes 49156
  7.2 113.7 %all-reduce.5.cloned.1.call-start = ((), (), s32[]{:S(2)}) async-start(), calls=%async_computation | async-start | bytes 4194304 | tf_op jit(solution)/shard_map/psum | solution.py:50
  103.7 100.3 %all-gather.3.cloned.1.call-start = ((), (), s32[]{:S(2)}) async-start(), calls=%async_computation.2 | async-start | bytes 8650752 | tf_op jit(solution)/shard_map/all_gather | solution.py:13
  125.2 334.4 %all-reduce.7.cloned.1.call-start = ((), (), s32[]{:S(2)}) async-start(), calls=%async_computation.1 | async-start | bytes 8388608 | tf_op jit(solution)/shard_map/psum | solution.py:56
Sparse Core Ops, SparseCore 0:
  103.8 17.0 all-reduce.4
  125.4 78.5 all-gather.2
  292.9 166.7 all-reduce.6
